TPU v7x, 512 devices: a whole 4x8x8 slice. The times are simulated.
512 devices in a mesh: slab: 64 (over x, z, core), filt: 8 (over y).
Axes of the slice: x: 4, y: 8, z: 8, core: 2. Of those that a mesh axis runs over, the one named last changes fastest.
Arguments:
- volume: bfloat16 [128, 128, 16, 256], P('slab', 'filt'), may hold values from -6 to 6
- weights: bfloat16 [3, 3, 3, 128, 256], replicated, may hold values from -0.109375 to 0.109375
- out_error: bfloat16 [64, 256, 8, 128], P('slab', 'filt'), may hold values from -6 to 6
Outputs:
- in_grad: bfloat16 [128, 128, 16, 256], P('slab', None, 'filt')
- weight_grad: float32 [3, 3, 3, 128, 256], P(None, None, None, None, 'filt')
All inputs are finite; a program needn't handle non-finite values.
Results may differ from a plain program's by a relative error of at most 0.0049.
Values may be sent and summed in bfloat16 or wider, within the bound.
No kernel may reach another device: no remote copies, remote signals or barrier semaphores. Data moves between devices by JAX's collectives and lax.ppermute only.
A program may use at most 64 MiB of HBM per device.

v0:
```python
import math
import jax
import jax.numpy as jnp
from jax import lax
from jax.sharding import PartitionSpec as P


def shifted_2(value, axis, steps):
    count = lax.axis_size(axis)
    first, last = (max(0, -steps), min(count, count - steps))
    return lax.ppermute(value, axis, [(source, source + steps) for source in range(first, last)])


def tap_pieces(extended, top):
    depth = (extended.shape[0] - 1) // 2
    rows = (extended.shape[2] + top - 1) // 2
    cols = extended.shape[3] // 2
    chans = extended.shape[1]
    padded = jnp.pad(extended, ((0, 1), (0, 0), (top, 1), (1, 1)))
    split = padded.reshape(depth + 1, 2, chans, rows + 1, 2, cols + 1, 2)
    pieces = []
    for a in range(3):
        for b in range(3):
            for c in range(3):
                piece = split[
                    a // 2 : a // 2 + depth,
                    a % 2,
                    :,
                    b // 2 : b // 2 + rows,
                    b % 2,
                    c // 2 : c // 2 + cols,
                    c % 2,
                ]
                pieces.append(((a, b, c), piece))
    return pieces


def forward_taps(pieces, kernel):
    total = None
    for (a, b, c), piece in pieces:
        term = jnp.einsum(
            "dkhw,kf->dfhw", piece, kernel[a, b, c], preferred_element_type=jnp.float32
        )
        total = term if total is None else total + term
    return total


def weight_taps(pieces, grad):
    terms = []
    for (a, b, c), piece in pieces:
        terms.append(jnp.einsum("dkhw,dfhw->kf", piece, grad, preferred_element_type=jnp.float32))
    stacked = jnp.stack(terms, 0)
    return stacked.reshape((3, 3, 3) + stacked.shape[1:])


def input_taps(grad_ext, kernel):
    depth = grad_ext.shape[0] - 1
    rows = grad_ext.shape[2] - 1
    cols = grad_ext.shape[3]
    chans = kernel.shape[3]
    parity_taps = ((1,), (2, 0))
    shifted = {}
    for a in range(3):
        for b in range(3):
            for c in range(3):
                term = jnp.einsum(
                    "dfhw,kf->dkhw", grad_ext, kernel[a, b, c], preferred_element_type=jnp.float32
                )
                start_d = 1 if a == 0 else 0
                start_r = 1 if b == 0 else 0
                term = term[start_d : start_d + depth, :, start_r : start_r + rows]
                if c == 0:
                    term = jnp.pad(term[..., 1:], ((0, 0), (0, 0), (0, 0), (0, 1)))
                shifted[a, b, c] = term
    depth_parts = []
    for even_d in range(2):
        row_parts = []
        for even_r in range(2):
            col_parts = []
            for even_c in range(2):
                total = None
                for a in parity_taps[even_d]:
                    for b in parity_taps[even_r]:
                        for c in parity_taps[even_c]:
                            total = shifted[a, b, c] if total is None else total + shifted[a, b, c]
                col_parts.append(total)
            row_parts.append(jnp.stack(col_parts, -1))
        row_parts = jnp.stack(row_parts, 3)
        depth_parts.append(row_parts)
    joined = jnp.stack(depth_parts, 1)
    return joined.reshape(2 * depth, chans, 2 * rows, 2 * cols)


def activation_grad(preact, error):
    sigma = jax.nn.sigmoid(preact)
    return (error * (sigma * (1.0 + preact * (1.0 - sigma)))).astype(jnp.bfloat16)


def on_device(volume, weights, out_error):
    member = lax.axis_index("filt")
    tile = out_error.shape[1]
    below = shifted_2(volume[-1:], "slab", 1)
    extended = jnp.concatenate([below, volume], 0)
    whole = lax.all_gather(extended, "filt", axis=1, tiled=True)
    pieces = tap_pieces(whole, 1)
    kernel_tile = lax.dynamic_slice_in_dim(weights, member * tile, tile, 4)
    preact = forward_taps(pieces, kernel_tile)
    grad = activation_grad(preact, out_error)
    weight_part = weight_taps(pieces, grad)
    grad_rows = lax.all_to_all(grad, "filt", split_axis=2, concat_axis=1, tiled=True)
    count = out_error.shape[0] * lax.axis_size("slab") * out_error.shape[2] * out_error.shape[3]
    weight_grad = lax.psum(weight_part, "slab") * (1.0 / math.sqrt(count))
    upper = shifted_2(grad_rows, "slab", -1)
    grad_ext = jnp.concatenate([grad_rows, upper], 0)
    right_row = shifted_2(grad_ext, "filt", -1)
    grad_ext = jnp.concatenate([grad_ext, right_row], 2)
    in_grad = input_taps(grad_ext, weights).astype(jnp.bfloat16)
    return (in_grad, weight_grad)


def solution(mesh):
    in_specs = (P("slab", "filt", None, None), P(), P("slab", "filt", None, None))
    out_specs = (P("slab", None, "filt", None), P(None, None, None, None, "filt"))
    return jax.shard_map(
        on_device, mesh=mesh, in_specs=in_specs, out_specs=out_specs, check_vma=False
    )
```

profile of v0, /device:TPU:1, one launch (start us, length us, event | category | flops | bytes accessed | tf_op | source)
XLA Modules:
  0.0 422.1 jit_solution(12113445541933201036)
XLA Ops:
  8.1 5.4 %collective-permute-start = (bf16[1,16,16,256]{3,2,1,0:T(8,128)(2,1)S(1)}, bf16[1,16,16,256]{3,2,1,0:T(8,128)(2,1)S(1)}, u32[]{:S(2)}, u32[]{:S(2)}) collective-permute-start(bf16[1,16,16,256]{3,2,1,0:T(8,128)(2,1)S(1)} %slice.347), channel_id=1, source_target_pairs={{0,8},{8,16},{16,24},{24,32},{32,40},{40,48},{48,56},{56,64},{64,7... | collective-permute-start | bytes 393224 | tf_op jit(solution)/shard_map/ppermute | solution.py:11
  13.5 3.6 collective-permute-done
  17.1 1.7 pad_maximum_fusion
  18.9 51.0 %all-gather.2.cloned.1.call-done = bf16[3,128,16,256]{3,2,1,0:T(8,128)(2,1)} async-done(((bf16[3,16,16,256]{3,2,1,0:T(8,128)(2,1)}), bf16[3,128,16,256]{3,2,1,0:T(8,128)(2,1)}) %all-gather.2.cloned.1.call-update) | async-done | bytes 3145744 | tf_op jit(solution)/shard_map/all_gather | solution.py:104
  69.9 6.1 %copy.203 = bf16[3,128,16,256]{1,0,3,2:T(4,128)(2,1)} copy(bf16[3,128,16,256]{3,2,1,0:T(8,128)(2,1)} %all-gather.2.cloned.1.call-done) | data formatting | bytes 6291456
  76.0 3.9 pad.32.clone
  79.9 4.1 fusion.214
  84.0 11.3 %fusion.213 = (bf16[1,1,128,8,1,128,1]{2,1,0,6,5,4,3:T(2,128)(2,1)}, bf16[1,1,128,8,1,128,1]{2,1,0,6,5,4,3:T(2,128)(2,1)}, bf16[1,1,128,8,1,128,1]{2,1,0,6,5,4,3...) fusion(bf16[2,2,128,9,2,129,2]{2,1,0,6,5,4,3:T(2,128)(2,1)S(1)}, ...), kind=kLoop, calls=%fused_computation.343 | loop fusion | bytes 9961472 | tf_op jit(solution)/shard_map/slice | solution.py:25
  96.2 1.3 copy.160
  97.4 1.9 copy.158
  99.3 1.9 copy.156
  101.2 1.9 copy.154
  103.0 1.9 copy.152
  104.9 1.9 copy.150
  106.8 1.9 copy.202
  110.0 1.3 copy.198
  111.2 1.3 copy.196
  112.9 1.3 copy.192
  114.6 1.3 copy.188
  116.3 1.3 copy.184
  117.6 1.3 copy.182
  118.8 1.9 copy.180
  120.7 1.9 copy.178
  122.6 1.9 copy.176
  124.5 1.9 copy.174
  126.3 1.9 copy.172
  128.2 1.9 copy.170
  130.1 1.9 copy.168
  132.0 1.9 copy.166
  136.4 1.3 convolution_add_fusion.24
  162.3 1.7 fusion.83
  164.0 1.6 fusion.27
  165.6 4.6 %all-to-all-start = ((bf16[1,32,8,128]{3,1,0,2:T(8,128)(2,1)}), bf16[1,32,8,128]{3,1,0,2:T(8,128)(2,1)S(1)}, u32[]{:S(2)}, u32[]{:S(2)}) async-start(bf16[1,32,8,128]{3,1,0,2:T(8,128)(2,1)} %bitcast.83), calls=%async_computation | async-start | bytes 131072 | tf_op jit(solution)/shard_map/all_to_all | solution.py:110
  170.5 1.8 fusion.26
  172.4 1.8 fusion.25
  174.2 1.8 fusion.24
  176.0 1.8 fusion.23
  177.8 1.7 fusion.22
  179.5 1.6 fusion.21
  181.1 1.6 fusion.20
  182.7 1.6 fusion.19
  184.4 1.6 fusion.18
  186.0 1.6 fusion.17
  187.7 1.6 fusion.16
  189.3 1.6 fusion.15
  191.0 1.6 fusion.14
  192.6 1.6 fusion.13
  194.3 1.6 fusion.12
  195.9 1.7 fusion.11
  197.6 1.6 fusion.10
  199.2 1.6 fusion.9
  200.9 1.6 fusion.8
  202.5 1.6 fusion.7
  204.2 1.6 fusion.6
  205.8 1.6 fusion.5
  207.5 1.8 fusion.4
  209.2 1.6 fusion.3
  210.9 1.6 fusion.2
  212.5 1.6 fusion.1
  214.3 3.0 collective-permute-start.1
  217.3 3.2 collective-permute-done.1
  220.5 1.3 collective-permute-start.2
  221.8 183.9 %all-reduce.12.cloned.1.call-done = f32[3,3,3,128,32]{3,4,2,1,0:T(8,128)} async-done(((f32[3,3,3,128,32]{3,4,2,1,0:T(8,128)}), f32[3,3,3,128,32]{3,4,2,1,0:T(8,128)}) %all-reduce.12.cloned.1.call-update) | async-done | bytes 442384 | tf_op jit(solution)/shard_map/psum | solution.py:112
  405.7 1.8 broadcast_multiply_fusion
  (135 shorter events, 38.8 us)
Async XLA Ops:
  7.2 62.7 %all-gather.2.cloned.1.call-start = ((), (), s32[]{:S(2)}) async-start(), calls=%async_computation.1 | async-start | bytes 3538944 | tf_op jit(solution)/shard_map/all_gather | solution.py:104
  8.1 9.0 %collective-permute-start = (bf16[1,16,16,256]{3,2,1,0:T(8,128)(2,1)S(1)}, bf16[1,16,16,256]{3,2,1,0:T(8,128)(2,1)S(1)}, u32[]{:S(2)}, u32[]{:S(2)}) collective-permute-start(bf16[1,16,16,256]{3,2,1,0:T(8,128)(2,1)S(1)} %slice.347), channel_id=1, source_target_pairs={{0,8},{8,16},{16,24},{24,32},{32,40},{40,48},{48,56},{56,64},{64,7... | collective-permute-start | bytes 393224 | tf_op jit(solution)/shard_map/ppermute | solution.py:11
  133.8 5.1 %copy-start = (bf16[1,1,128,8,1,128,1]{5,2,3,6,4,1,0:T(8,128)(2,1)S(1)}, bf16[1,1,128,8,1,128,1]{5,2,3,6,4,1,0:T(8,128)(2,1)}, u32[]{:S(2)}) copy-start(bf16[1,1,128,8,1,128,1]{5,2,3,6,4,1,0:T(8,128)(2,1)} %copy.158) | copy-start | bytes 786436
  136.4 7.0 %copy-start.16 = (bf16[1,1,128,8,1,128,1]{5,2,3,6,4,1,0:T(8,128)(2,1)S(1)}, bf16[1,1,128,8,1,128,1]{5,2,3,6,4,1,0:T(8,128)(2,1)}, u32[]{:S(2)}) copy-start(bf16[1,1,128,8,1,128,1]{5,2,3,6,4,1,0:T(8,128)(2,1)} %copy.166) | copy-start | bytes 786436
  137.7 6.8 %copy-start.14 = (bf16[1,1,128,8,1,128,1]{5,2,3,6,4,1,0:T(8,128)(2,1)S(1)}, bf16[1,1,128,8,1,128,1]{5,2,3,6,4,1,0:T(8,128)(2,1)}, u32[]{:S(2)}) copy-start(bf16[1,1,128,8,1,128,1]{5,2,3,6,4,1,0:T(8,128)(2,1)} %copy.168) | copy-start | bytes 786436
  139.0 6.5 %copy-start.11 = (bf16[1,1,128,8,1,128,1]{5,2,3,6,4,1,0:T(8,128)(2,1)S(1)}, bf16[1,1,128,8,1,128,1]{5,2,3,6,4,1,0:T(8,128)(2,1)}, u32[]{:S(2)}) copy-start(bf16[1,1,128,8,1,128,1]{5,2,3,6,4,1,0:T(8,128)(2,1)} %copy.170) | copy-start | bytes 786436
  140.1 6.5 %copy-start.9 = (bf16[1,1,128,8,1,128,1]{5,2,3,6,4,1,0:T(8,128)(2,1)S(1)}, bf16[1,1,128,8,1,128,1]{5,2,3,6,4,1,0:T(8,128)(2,1)}, u32[]{:S(2)}) copy-start(bf16[1,1,128,8,1,128,1]{5,2,3,6,4,1,0:T(8,128)(2,1)} %copy.172) | copy-start | bytes 786436
  141.1 6.5 %copy-start.7 = (bf16[1,1,128,8,1,128,1]{5,2,3,6,4,1,0:T(8,128)(2,1)S(1)}, bf16[1,1,128,8,1,128,1]{5,2,3,6,4,1,0:T(8,128)(2,1)}, u32[]{:S(2)}) copy-start(bf16[1,1,128,8,1,128,1]{5,2,3,6,4,1,0:T(8,128)(2,1)} %copy.174) | copy-start | bytes 786436
  142.2 6.4 %copy-start.5 = (bf16[1,1,128,8,1,128,1]{5,2,3,6,4,1,0:T(8,128)(2,1)S(1)}, bf16[1,1,128,8,1,128,1]{5,2,3,6,4,1,0:T(8,128)(2,1)}, u32[]{:S(2)}) copy-start(bf16[1,1,128,8,1,128,1]{5,2,3,6,4,1,0:T(8,128)(2,1)} %copy.176) | copy-start | bytes 786436
  143.3 6.4 %copy-start.3 = (bf16[1,1,128,8,1,128,1]{5,2,3,6,4,1,0:T(8,128)(2,1)S(1)}, bf16[1,1,128,8,1,128,1]{5,2,3,6,4,1,0:T(8,128)(2,1)}, u32[]{:S(2)}) copy-start(bf16[1,1,128,8,1,128,1]{5,2,3,6,4,1,0:T(8,128)(2,1)} %copy.178) | copy-start | bytes 786436
  144.4 6.3 %copy-start.1 = (bf16[1,1,128,8,1,128,1]{5,2,3,6,4,1,0:T(8,128)(2,1)S(1)}, bf16[1,1,128,8,1,128,1]{5,2,3,6,4,1,0:T(8,128)(2,1)}, u32[]{:S(2)}) copy-start(bf16[1,1,128,8,1,128,1]{5,2,3,6,4,1,0:T(8,128)(2,1)} %copy.180) | copy-start | bytes 786436
  155.9 6.3 %copy-start.18 = (bf16[1,1,128,8,1,128,1]{5,2,3,6,4,1,0:T(8,128)(2,1)S(1)}, bf16[1,1,128,8,1,128,1]{5,2,3,6,4,1,0:T(8,128)(2,1)}, u32[]{:S(2)}) copy-start(bf16[1,1,128,8,1,128,1]{5,2,3,6,4,1,0:T(8,128)(2,1)} %copy.202) | copy-start | bytes 786436
  155.9 6.3 %copy-start.21 = (bf16[1,32,8,128]{3,2,1,0:T(8,128)(2,1)S(1)}, bf16[1,32,8,128]{3,2,1,0:T(8,128)(2,1)}, u32[]{:S(2)}) copy-start(bf16[1,32,8,128]{3,2,1,0:T(8,128)(2,1)} %param.5) | copy-start | bytes 196612
  157.0 7.0 %copy-start.13 = (bf16[1,1,128,8,1,128,1]{5,2,3,6,4,1,0:T(8,128)(2,1)S(1)}, bf16[1,1,128,8,1,128,1]{5,2,3,6,4,1,0:T(8,128)(2,1)}, u32[]{:S(2)}) copy-start(bf16[1,1,128,8,1,128,1]{5,2,3,6,4,1,0:T(8,128)(2,1)} %copy.150) | copy-start | bytes 786436
  165.6 48.6 %all-to-all-start = ((bf16[1,32,8,128]{3,1,0,2:T(8,128)(2,1)}), bf16[1,32,8,128]{3,1,0,2:T(8,128)(2,1)S(1)}, u32[]{:S(2)}, u32[]{:S(2)}) async-start(bf16[1,32,8,128]{3,1,0,2:T(8,128)(2,1)} %bitcast.83), calls=%async_computation | async-start | bytes 131072 | tf_op jit(solution)/shard_map/all_to_all | solution.py:110
  170.3 235.4 %all-reduce.12.cloned.1.call-start = ((), (), s32[]{:S(2)}) async-start(), calls=%async_computation.2 | async-start | bytes 884736 | tf_op jit(solution)/shard_map/psum | solution.py:112
  170.5 12.3 %copy-start.17 = (bf16[1,1,128,8,1,128,1]{5,2,3,6,4,1,0:T(8,128)(2,1)S(1)}, bf16[1,1,128,8,1,128,1]{5,2,3,6,4,1,0:T(8,128)(2,1)}, u32[]{:S(2)}) copy-start(bf16[1,1,128,8,1,128,1]{5,2,3,6,4,1,0:T(8,128)(2,1)} %copy.166) | copy-start | bytes 786436
  170.5 13.9 %copy-start.15 = (bf16[1,1,128,8,1,128,1]{5,2,3,6,4,1,0:T(8,128)(2,1)S(1)}, bf16[1,1,128,8,1,128,1]{5,2,3,6,4,1,0:T(8,128)(2,1)}, u32[]{:S(2)}) copy-start(bf16[1,1,128,8,1,128,1]{5,2,3,6,4,1,0:T(8,128)(2,1)} %copy.168) | copy-start | bytes 786436
  170.5 15.5 %copy-start.12 = (bf16[1,1,128,8,1,128,1]{5,2,3,6,4,1,0:T(8,128)(2,1)S(1)}, bf16[1,1,128,8,1,128,1]{5,2,3,6,4,1,0:T(8,128)(2,1)}, u32[]{:S(2)}) copy-start(bf16[1,1,128,8,1,128,1]{5,2,3,6,4,1,0:T(8,128)(2,1)} %copy.170) | copy-start | bytes 786436
  170.5 17.2 %copy-start.10 = (bf16[1,1,128,8,1,128,1]{5,2,3,6,4,1,0:T(8,128)(2,1)S(1)}, bf16[1,1,128,8,1,128,1]{5,2,3,6,4,1,0:T(8,128)(2,1)}, u32[]{:S(2)}) copy-start(bf16[1,1,128,8,1,128,1]{5,2,3,6,4,1,0:T(8,128)(2,1)} %copy.172) | copy-start | bytes 786436
  172.4 17.0 %copy-start.8 = (bf16[1,1,128,8,1,128,1]{5,2,3,6,4,1,0:T(8,128)(2,1)S(1)}, bf16[1,1,128,8,1,128,1]{5,2,3,6,4,1,0:T(8,128)(2,1)}, u32[]{:S(2)}) copy-start(bf16[1,1,128,8,1,128,1]{5,2,3,6,4,1,0:T(8,128)(2,1)} %copy.174) | copy-start | bytes 786436
  174.2 16.8 %copy-start.6 = (bf16[1,1,128,8,1,128,1]{5,2,3,6,4,1,0:T(8,128)(2,1)S(1)}, bf16[1,1,128,8,1,128,1]{5,2,3,6,4,1,0:T(8,128)(2,1)}, u32[]{:S(2)}) copy-start(bf16[1,1,128,8,1,128,1]{5,2,3,6,4,1,0:T(8,128)(2,1)} %copy.176) | copy-start | bytes 786436
  176.0 16.7 %copy-start.4 = (bf16[1,1,128,8,1,128,1]{5,2,3,6,4,1,0:T(8,128)(2,1)S(1)}, bf16[1,1,128,8,1,128,1]{5,2,3,6,4,1,0:T(8,128)(2,1)}, u32[]{:S(2)}) copy-start(bf16[1,1,128,8,1,128,1]{5,2,3,6,4,1,0:T(8,128)(2,1)} %copy.178) | copy-start | bytes 786436
  177.8 16.5 %copy-start.2 = (bf16[1,1,128,8,1,128,1]{5,2,3,6,4,1,0:T(8,128)(2,1)S(1)}, bf16[1,1,128,8,1,128,1]{5,2,3,6,4,1,0:T(8,128)(2,1)}, u32[]{:S(2)}) copy-start(bf16[1,1,128,8,1,128,1]{5,2,3,6,4,1,0:T(8,128)(2,1)} %copy.180) | copy-start | bytes 786436
  195.9 16.6 %copy-start.19 = (bf16[1,1,128,8,1,128,1]{5,2,3,6,4,1,0:T(8,128)(2,1)S(1)}, bf16[1,1,128,8,1,128,1]{5,2,3,6,4,1,0:T(8,128)(2,1)}, u32[]{:S(2)}) copy-start(bf16[1,1,128,8,1,128,1]{5,2,3,6,4,1,0:T(8,128)(2,1)} %copy.202) | copy-start | bytes 786436
  207.5 200.0 %copy-start.20 = (bf16[3,3,3,128,256]{4,3,2,1,0:T(8,128)(2,1)S(1)}, bf16[3,3,3,128,256]{4,3,2,1,0:T(8,128)(2,1)}, u32[]{:S(2)}) copy-start(bf16[3,3,3,128,256]{4,3,2,1,0:T(8,128)(2,1)} %param.4) | copy-start | bytes 5308420
  214.3 6.1 %collective-permute-start.1 = (bf16[1,256,1,128]{1,3,2,0:T(8,128)(2,1)S(1)}, bf16[1,256,1,128]{1,3,2,0:T(8,128)(2,1)S(1)}, u32[]{:S(2)}, u32[]{:S(2)}) collective-permute-start(bf16[1,256,1,128]{1,3,2,0:T(8,128)(2,1)S(1)} %copy.115), channel_id=1, source_target_pairs={{8,0},{16,8},{24,16},{32,24},{40,32},{48,40},{56,48},{64,56},{72,6... | collective-permute-start | bytes 196616 | tf_op jit(solution)/shard_map/ppermute | solution.py:11
  220.5 187.0 %collective-permute-start.2 = (bf16[2,256,1,128]{1,3,2,0:T(8,128)(2,1)S(1)}, bf16[2,256,1,128]{1,3,2,0:T(8,128)(2,1)S(1)}, u32[]{:S(2)}, u32[]{:S(2)}) collective-permute-start(bf16[2,256,1,128]{1,3,2,0:T(8,128)(2,1)S(1)} %pad_maximum_fusion.2), channel_id=1, source_target_pairs={{1,0},{2,1},{3,2},{4,3},{5,4},{6,5},{7,6},{9,8},{10,9},{11,10},{12... | collective-permute-start | bytes 393224 | tf_op jit(solution)/shard_map/ppermute | solution.py:11
Sparse Core Ops, SparseCore 0:
  19.0 50.8 all-gather.1
  214.3 191.2 all-reduce.11
where the time goes:
time: 425 us; the launch traced here: 422 us
  waiting for transfers between devices  242 us (57%)
  matrix products  80.7 us (19%)
  local copies, waits for them, and re-layouts  66.4 us (16%)
  between operations  15 us (4%)
  starting transfers between devices  14.5 us (3%)
    psum x1, waiting for transfers between devices, on_device(): weight_grad = lax.psum(weight_part, 'slab') * (1.0 / math.sqrt(count))  184 us
    all_gather x1, waiting for transfers between devices, on_device(): whole = lax.all_gather(extended, 'filt', axis=1, tiled=True)  51 us
    unnamed x73, local copies, waits for them, and re-layouts  45.6 us
    dot_general x27, matrix products, weight_taps(): jnp.einsum('dkhw,dfhw->kf', piece, grad, preferred_element_type=jnp.float32)  45.2 us
    dot_general x27, matrix products, forward_taps(): jnp.einsum('dkhw,kf->dfhw', piece, kernel[a, b, c], preferred_element_typ...  29.6 us
    slice x2, local copies, waits for them, and re-layouts, tap_pieces(): split[a // 2:a // 2 + depth, a % 2, :, b // 2:b // 2 + rows, b % 2, c //...  15.4 us
    ppermute x3, starting transfers between devices, shifted_2(): lax.ppermute(value, axis, [(source, source + steps) for source in range(f...  9.64 us
  transfers between devices with their start and end apart: 6, of which 4 were waited for; matrix products, arithmetic and copies ran while one was open for 11% of the time, Pallas kernels for 0%

commit v1 on v0

--- a/solution.py
+++ b/solution.py
@@ -109,7 +109,7 @@
     weight_part = weight_taps(pieces, grad)
     grad_rows = lax.all_to_all(grad, "filt", split_axis=2, concat_axis=1, tiled=True)
     count = out_error.shape[0] * lax.axis_size("slab") * out_error.shape[2] * out_error.shape[3]
-    weight_grad = lax.psum(weight_part, "slab") * (1.0 / math.sqrt(count))
+    weight_grad = jnp.sum(lax.all_gather(weight_part, "slab"), axis=0) * (1.0 / math.sqrt(count))
     upper = shifted_2(grad_rows, "slab", -1)
     grad_ext = jnp.concatenate([grad_rows, upper], 0)
     right_row = shifted_2(grad_ext, "filt", -1)

time: 425 us -> 325 us (0.76)
  waiting for transfers between devices: 242 us -> 165 us
  matrix products: 80.7 us -> 40.4 us
  blocking collectives: 0 us -> 11.7 us
  other arithmetic: 3.77 us -> 12.7 us
    psum x1 -> x0, waiting for transfers between devices: 184 us -> none  [on_device(): weight_grad = lax.psum(weight_part, 'slab') * (1.0 / math.sqrt(count))]
    all_gather x0 -> x1, waiting for transfers between devices: none -> 101 us  [on_device(): lax.all_gather(weight_part, 'slab')]
    dot_general x27, matrix products: 45.2 us -> 5.36 us  [weight_taps(): jnp.einsum('dkhw,dfhw->kf', piece, grad, preferred_element_type=jnp.float32)]
    all_to_all x0 -> x1, blocking collectives: none -> 11.7 us  [on_device(): lax.all_to_all(grad, 'filt', split_axis=2, concat_axis=1, tiled=True)]
    reduce_sum x0 -> x1, other arithmetic: none -> 10 us  [on_device(): jnp.sum(lax.all_gather(weight_part, 'slab'), axis=0)]
    ppermute x3, waiting for transfers between devices: 6.79 us -> 13.3 us  [shifted_2(): lax.ppermute(value, axis, [(source, source + steps) for source in range(f...]
    all_to_all x1 -> x0, starting transfers between devices: 4.63 us -> none  [on_device(): lax.all_to_all(grad, 'filt', split_axis=2, concat_axis=1, tiled=True)]
    unnamed x73 -> x63, local copies, waits for them, and re-layouts: 45.6 us -> 45.6 us
  transfers between devices with their start and end apart: 6 -> 5, of which waited for: 4 -> 5; matrix products, arithmetic and copies ran while one was open for 11% -> 2% of each run, Pallas kernels for 0% -> 0%
where the time goes in v1:
time: 325 us; the launch traced here: 323 us
  waiting for transfers between devices  165 us (51%)
  local copies, waits for them, and re-layouts  66.9 us (21%)
  matrix products  40.4 us (12%)
  between operations  15 us (5%)
  other arithmetic  12.7 us (4%)
  blocking collectives  11.7 us (4%)
  starting transfers between devices  10.9 us (3%)
    all_gather x1, waiting for transfers between devices, on_device(): lax.all_gather(weight_part, 'slab')  101 us
    all_gather x1, waiting for transfers between devices, on_device(): whole = lax.all_gather(extended, 'filt', axis=1, tiled=True)  50.9 us
    unnamed x63, local copies, waits for them, and re-layouts  45.6 us
    dot_general x27, matrix products, forward_taps(): jnp.einsum('dkhw,kf->dfhw', piece, kernel[a, b, c], preferred_element_typ...  29 us
    slice x2, local copies, waits for them, and re-layouts, tap_pieces(): split[a // 2:a // 2 + depth, a % 2, :, b // 2:b // 2 + rows, b % 2, c //...  15.9 us
    ppermute x3, waiting for transfers between devices, shifted_2(): lax.ppermute(value, axis, [(source, source + steps) for source in range(f...  13.3 us
    all_to_all x1, blocking collectives, on_device(): lax.all_to_all(grad, 'filt', split_axis=2, concat_axis=1, tiled=True)  11.7 us
    ppermute x3, starting transfers between devices, shifted_2(): lax.ppermute(value, axis, [(source, source + steps) for source in range(f...  10.8 us
  transfers between devices with their start and end apart: 5, of which 5 were waited for; matrix products, arithmetic and copies ran while one was open for 2% of the time, Pallas kernels for 0%

profile of v1, /device:TPU:1, one launch (start us, length us, event | category | flops | bytes accessed | tf_op | source)
XLA Modules:
  0.0 322.6 jit_solution(17634800715958294785)
XLA Ops:
  7.2 0.9 slice.347
  8.1 5.4 %collective-permute-start = (bf16[1,16,16,256]{3,2,1,0:T(8,128)(2,1)S(1)}, bf16[1,16,16,256]{3,2,1,0:T(8,128)(2,1)S(1)}, u32[]{:S(2)}, u32[]{:S(2)}) collective-permute-start(bf16[1,16,16,256]{3,2,1,0:T(8,128)(2,1)S(1)} %slice.347), channel_id=1, source_target_pairs={{0,8},{8,16},{16,24},{24,32},{32,40},{40,48},{48,56},{56,64},{64,7... | collective-permute-start | bytes 393224 | tf_op jit(solution)/shard_map/ppermute | solution.py:11
  13.5 3.6 %collective-permute-done = bf16[1,16,16,256]{3,2,1,0:T(8,128)(2,1)S(1)} collective-permute-done((bf16[1,16,16,256]{3,2,1,0:T(8,128)(2,1)S(1)}, bf16[1,16,16,256]{3,2,1,0:T(8,128)(2,1)S(1)}, u32[]{:S(2)}, u32[]{:S(2)}) %collective-permute-start) | collective-permute-done | bytes 131104 | tf_op jit(solution)/shard_map/ppermute | solution.py:11
  17.1 1.7 pad_maximum_fusion
  18.9 50.9 %all-gather.3.cloned.1.call-done = bf16[3,128,16,256]{3,2,1,0:T(8,128)(2,1)} async-done(((bf16[3,16,16,256]{3,2,1,0:T(8,128)(2,1)}), bf16[3,128,16,256]{3,2,1,0:T(8,128)(2,1)}) %all-gather.3.cloned.1.call-update) | async-done | bytes 3145744 | tf_op jit(solution)/shard_map/all_gather | solution.py:104
  69.9 6.2 %copy.203 = bf16[3,128,16,256]{1,0,3,2:T(4,128)(2,1)} copy(bf16[3,128,16,256]{3,2,1,0:T(8,128)(2,1)} %all-gather.3.cloned.1.call-done) | data formatting | bytes 6291456
  76.0 3.9 %pad.32.clone = bf16[4,128,18,258]{1,0,3,2:T(4,128)(2,1)S(1)} pad(bf16[3,128,16,256]{1,0,3,2:T(4,128)(2,1)} %copy.203, bf16[]{:T(256)} %constant.16.clone.1), padding=0_1x0_0x1_1x1_1 | pad | bytes 7901186 | tf_op jit(solution)/shard_map/jit(_pad)/pad | solution.py:19
  80.0 4.9 %fusion.214 = (bf16[1,1,128,8,1,128,1]{2,1,0,6,5,4,3:T(2,128)(2,1)}, bf16[1,1,128,8,1,128,1]{2,1,0,6,5,4,3:T(2,128)(2,1)}, bf16[1,1,128,8,1,128,1]{2,1,0,6,5,4,3...) fusion(bf16[2,2,128,9,2,129,2]{2,1,0,6,5,4,3:T(2,128)(2,1)S(1)}, ...), kind=kLoop, calls=%fused_computation.344 | loop fusion | bytes 4194304 | tf_op jit(solution)/shard_map/slice | solution.py:25
  84.9 11.0 %fusion.213 = (bf16[1,1,128,8,1,128,1]{2,1,0,6,5,4,3:T(2,128)(2,1)}, bf16[1,1,128,8,1,128,1]{2,1,0,6,5,4,3:T(2,128)(2,1)}, bf16[1,1,128,8,1,128,1]{2,1,0,6,5,4,3...) fusion(bf16[2,2,128,9,2,129,2]{2,1,0,6,5,4,3:T(2,128)(2,1)S(1)}, ...), kind=kLoop, calls=%fused_computation.343 | loop fusion | bytes 9961472 | tf_op jit(solution)/shard_map/slice | solution.py:25
  95.9 1.9 copy.150
  97.8 1.9 copy.152
  99.7 1.9 copy.154
  101.5 1.9 copy.156
  103.4 1.9 copy.158
  105.3 1.9 copy.160
  107.2 1.9 copy.162
  109.0 1.9 copy.164
  110.9 1.9 copy.166
  112.8 1.9 copy.168
  114.7 1.9 copy.170
  116.6 1.9 copy.172
  118.5 1.9 copy.174
  120.7 1.3 copy.178
  122.4 1.3 copy.182
  124.1 1.3 copy.186
  125.8 1.3 copy.190
  127.4 1.3 copy.194
  129.1 1.3 copy.198
  130.4 1.3 copy.200
  131.7 1.9 copy.202
  133.6 1.3 fusion.81
  134.9 1.3 convolution_add_fusion.25
  136.2 1.3 convolution_add_fusion.24
  137.5 1.3 convolution_add_fusion.23
  138.8 1.1 convolution_add_fusion.22
  139.9 1.1 convolution_add_fusion.21
  141.0 1.1 convolution_add_fusion.20
  142.1 1.0 convolution_add_fusion.19
  143.1 1.0 convolution_add_fusion.18
  144.2 1.0 convolution_add_fusion.17
  145.2 1.0 convolution_add_fusion.16
  146.3 1.0 convolution_add_fusion.15
  147.3 1.0 convolution_add_fusion.14
  148.3 1.0 convolution_add_fusion.13
  149.4 1.0 convolution_add_fusion.12
  150.4 1.0 convolution_add_fusion.11
  151.4 1.0 convolution_add_fusion.10
  152.5 1.0 convolution_add_fusion.9
  153.5 1.0 convolution_add_fusion.8
  154.5 1.0 convolution_add_fusion.7
  155.6 1.1 convolution_add_fusion.6
  156.7 1.1 convolution_add_fusion.5
  157.8 1.1 convolution_add_fusion.4
  158.9 1.1 convolution_add_fusion.3
  160.0 1.0 convolution_add_fusion.2
  161.0 1.0 convolution_add_fusion.1
  162.1 1.1 fusion.83
  169.3 11.7 %all_to_all.18 = bf16[1,32,8,128]{3,1,0,2:T(8,128)(2,1)S(1)} all-to-all(bf16[1,32,8,128]{3,1,0,2:T(8,128)(2,1)S(1)} %bitcast.766), channel_id=1, replica_groups=mesh['slab'=64,'filt'=8] {'filt'}, dimensions={2} | all-to-all | bytes 131072 | tf_op jit(solution)/shard_map/all_to_all | solution.py:110
  181.1 4.1 %collective-permute-start.1 = (bf16[1,256,1,128]{1,3,2,0:T(8,128)(2,1)S(1)}, bf16[1,256,1,128]{1,3,2,0:T(8,128)(2,1)S(1)}, u32[]{:S(2)}, u32[]{:S(2)}) collective-permute-start(bf16[1,256,1,128]{1,3,2,0:T(8,128)(2,1)S(1)} %copy.115), channel_id=1, source_target_pairs={{8,0},{16,8},{24,16},{32,24},{40,32},{48,40},{56,48},{64,56},{72,6... | collective-permute-start | bytes 196616 | tf_op jit(solution)/shard_map/ppermute | solution.py:11
  185.2 4.9 %collective-permute-done.1 = bf16[1,256,1,128]{1,3,2,0:T(8,128)(2,1)S(1)} collective-permute-done((bf16[1,256,1,128]{1,3,2,0:T(8,128)(2,1)S(1)}, bf16[1,256,1,128]{1,3,2,0:T(8,128)(2,1)S(1)}, u32[]{:S(2)}, u32[]{:S(2)}) %collective-permute-start.1) | collective-permute-done | bytes 65568 | tf_op jit(solution)/shard_map/ppermute | solution.py:11
  190.1 1.3 collective-permute-start.2
  191.4 4.8 %collective-permute-done.2 = bf16[2,256,1,128]{1,3,2,0:T(8,128)(2,1)S(1)} collective-permute-done((bf16[2,256,1,128]{1,3,2,0:T(8,128)(2,1)S(1)}, bf16[2,256,1,128]{1,3,2,0:T(8,128)(2,1)S(1)}, u32[]{:S(2)}, u32[]{:S(2)}) %collective-permute-start.2) | collective-permute-done | bytes 131104 | tf_op jit(solution)/shard_map/ppermute | solution.py:11
  204.1 100.8 %all-gather.5.cloned.1.call-done = f32[64,3,3,3,128,32]{4,5,3,2,1,0:T(8,128)} async-done(((f32[1,3,3,3,128,32]{4,5,3,2,1,0:T(8,128)}), f32[64,3,3,3,128,32]{4,5,3,2,1,0:T(8,128)}) %all-gather.5.cloned.1.call-update) | async-done | bytes 28311568 | tf_op jit(solution)/shard_map/all_gather | solution.py:112
  304.9 10.0 %reduce_sum.9 = f32[3,3,3,128,32]{3,4,2,1,0:T(8,128)S(1)} reduce(f32[64,3,3,3,128,32]{4,5,3,2,1,0:T(8,128)} %all-gather.5.cloned.1.call-done, f32[]{:T(128)} %constant.17.clone.1), dimensions={0}, to_apply=%region_0.1 | reduce | flops 6967296 | bytes 28753924 | tf_op jit(solution)/shard_map/reduce_sum | solution.py:112
  (125 shorter events, 17.2 us)
Async XLA Ops:
  7.2 62.7 %all-gather.3.cloned.1.call-start = ((), (), s32[]{:S(2)}) async-start(), calls=%async_computation.1 | async-start | bytes 3538944 | tf_op jit(solution)/shard_map/all_gather | solution.py:104
  8.1 9.0 %collective-permute-start = (bf16[1,16,16,256]{3,2,1,0:T(8,128)(2,1)S(1)}, bf16[1,16,16,256]{3,2,1,0:T(8,128)(2,1)S(1)}, u32[]{:S(2)}, u32[]{:S(2)}) collective-permute-start(bf16[1,16,16,256]{3,2,1,0:T(8,128)(2,1)S(1)} %slice.347), channel_id=1, source_target_pairs={{0,8},{8,16},{16,24},{24,32},{32,40},{40,48},{48,56},{56,64},{64,7... | collective-permute-start | bytes 393224 | tf_op jit(solution)/shard_map/ppermute | solution.py:11
  18.9 286.0 %all-gather.5.cloned.1.call-start = ((), (), s32[]{:S(2)}) async-start(), calls=%async_computation.2 | async-start | bytes 28753920 | tf_op jit(solution)/shard_map/all_gather | solution.py:112
  133.6 5.2 %copy-start.8 = (bf16[1,1,128,8,1,128,1]{5,2,3,6,4,1,0:T(8,128)(2,1)S(1)}, bf16[1,1,128,8,1,128,1]{5,2,3,6,4,1,0:T(8,128)(2,1)}, u32[]{:S(2)}) copy-start(bf16[1,1,128,8,1,128,1]{5,2,3,6,4,1,0:T(8,128)(2,1)} %copy.158) | copy-start | bytes 786436
  133.6 6.3 %copy-start.7 = (bf16[1,1,128,8,1,128,1]{5,2,3,6,4,1,0:T(8,128)(2,1)S(1)}, bf16[1,1,128,8,1,128,1]{5,2,3,6,4,1,0:T(8,128)(2,1)}, u32[]{:S(2)}) copy-start(bf16[1,1,128,8,1,128,1]{5,2,3,6,4,1,0:T(8,128)(2,1)} %copy.160) | copy-start | bytes 786436
  133.6 7.4 %copy-start.5 = (bf16[1,1,128,8,1,128,1]{5,2,3,6,4,1,0:T(8,128)(2,1)S(1)}, bf16[1,1,128,8,1,128,1]{5,2,3,6,4,1,0:T(8,128)(2,1)}, u32[]{:S(2)}) copy-start(bf16[1,1,128,8,1,128,1]{5,2,3,6,4,1,0:T(8,128)(2,1)} %copy.162) | copy-start | bytes 786436
  134.9 7.2 %copy-start.6 = (bf16[1,1,128,8,1,128,1]{5,2,3,6,4,1,0:T(8,128)(2,1)S(1)}, bf16[1,1,128,8,1,128,1]{5,2,3,6,4,1,0:T(8,128)(2,1)}, u32[]{:S(2)}) copy-start(bf16[1,1,128,8,1,128,1]{5,2,3,6,4,1,0:T(8,128)(2,1)} %copy.164) | copy-start | bytes 786436
  136.2 7.0 %copy-start.4 = (bf16[1,1,128,8,1,128,1]{5,2,3,6,4,1,0:T(8,128)(2,1)S(1)}, bf16[1,1,128,8,1,128,1]{5,2,3,6,4,1,0:T(8,128)(2,1)}, u32[]{:S(2)}) copy-start(bf16[1,1,128,8,1,128,1]{5,2,3,6,4,1,0:T(8,128)(2,1)} %copy.166) | copy-start | bytes 786436
  137.5 6.7 %copy-start.3 = (bf16[1,1,128,8,1,128,1]{5,2,3,6,4,1,0:T(8,128)(2,1)S(1)}, bf16[1,1,128,8,1,128,1]{5,2,3,6,4,1,0:T(8,128)(2,1)}, u32[]{:S(2)}) copy-start(bf16[1,1,128,8,1,128,1]{5,2,3,6,4,1,0:T(8,128)(2,1)} %copy.168) | copy-start | bytes 786436
  138.8 6.4 %copy-start.2 = (bf16[1,1,128,8,1,128,1]{5,2,3,6,4,1,0:T(8,128)(2,1)S(1)}, bf16[1,1,128,8,1,128,1]{5,2,3,6,4,1,0:T(8,128)(2,1)}, u32[]{:S(2)}) copy-start(bf16[1,1,128,8,1,128,1]{5,2,3,6,4,1,0:T(8,128)(2,1)} %copy.170) | copy-start | bytes 786436
  139.9 6.4 %copy-start.1 = (bf16[1,1,128,8,1,128,1]{5,2,3,6,4,1,0:T(8,128)(2,1)S(1)}, bf16[1,1,128,8,1,128,1]{5,2,3,6,4,1,0:T(8,128)(2,1)}, u32[]{:S(2)}) copy-start(bf16[1,1,128,8,1,128,1]{5,2,3,6,4,1,0:T(8,128)(2,1)} %copy.172) | copy-start | bytes 786436
  141.0 6.3 %copy-start = (bf16[1,1,128,8,1,128,1]{5,2,3,6,4,1,0:T(8,128)(2,1)S(1)}, bf16[1,1,128,8,1,128,1]{5,2,3,6,4,1,0:T(8,128)(2,1)}, u32[]{:S(2)}) copy-start(bf16[1,1,128,8,1,128,1]{5,2,3,6,4,1,0:T(8,128)(2,1)} %copy.174) | copy-start | bytes 786436
  155.6 6.5 %copy-start.13 = (bf16[1,1,128,8,1,128,1]{5,2,3,6,4,1,0:T(8,128)(2,1)S(1)}, bf16[1,1,128,8,1,128,1]{5,2,3,6,4,1,0:T(8,128)(2,1)}, u32[]{:S(2)}) copy-start(bf16[1,1,128,8,1,128,1]{5,2,3,6,4,1,0:T(8,128)(2,1)} %copy.202) | copy-start | bytes 786436
  155.6 6.5 %copy-start.16 = (bf16[1,32,8,128]{3,2,1,0:T(8,128)(2,1)S(1)}, bf16[1,32,8,128]{3,2,1,0:T(8,128)(2,1)}, u32[]{:S(2)}) copy-start(bf16[1,32,8,128]{3,2,1,0:T(8,128)(2,1)} %param.5) | copy-start | bytes 196612
  156.7 6.5 %copy-start.11 = (bf16[1,1,128,8,1,128,1]{5,2,3,6,4,1,0:T(8,128)(2,1)S(1)}, bf16[1,1,128,8,1,128,1]{5,2,3,6,4,1,0:T(8,128)(2,1)}, u32[]{:S(2)}) copy-start(bf16[1,1,128,8,1,128,1]{5,2,3,6,4,1,0:T(8,128)(2,1)} %copy.150) | copy-start | bytes 786436
  157.8 5.6 %copy-start.12 = (bf16[1,1,128,8,1,128,1]{5,2,3,6,4,1,0:T(8,128)(2,1)S(1)}, bf16[1,1,128,8,1,128,1]{5,2,3,6,4,1,0:T(8,128)(2,1)}, u32[]{:S(2)}) copy-start(bf16[1,1,128,8,1,128,1]{5,2,3,6,4,1,0:T(8,128)(2,1)} %copy.152) | copy-start | bytes 786436
  158.8 4.7 %copy-start.10 = (bf16[1,1,128,8,1,128,1]{5,2,3,6,4,1,0:T(8,128)(2,1)S(1)}, bf16[1,1,128,8,1,128,1]{5,2,3,6,4,1,0:T(8,128)(2,1)}, u32[]{:S(2)}) copy-start(bf16[1,1,128,8,1,128,1]{5,2,3,6,4,1,0:T(8,128)(2,1)} %copy.154) | copy-start | bytes 786436
  158.9 4.9 %copy-start.9 = (bf16[1,1,128,8,1,128,1]{5,2,3,6,4,1,0:T(8,128)(2,1)S(1)}, bf16[1,1,128,8,1,128,1]{5,2,3,6,4,1,0:T(8,128)(2,1)}, u32[]{:S(2)}) copy-start(bf16[1,1,128,8,1,128,1]{5,2,3,6,4,1,0:T(8,128)(2,1)} %copy.156) | copy-start | bytes 786436
  167.1 29.1 %copy-start.15 = (bf16[3,3,3,128,256]{4,3,2,1,0:T(8,128)(2,1)S(1)}, bf16[3,3,3,128,256]{4,3,2,1,0:T(8,128)(2,1)}, u32[]{:S(2)}) copy-start(bf16[3,3,3,128,256]{4,3,2,1,0:T(8,128)(2,1)} %param.4) | copy-start | bytes 5308420
  168.5 0.8 copy-start.14
  181.1 9.0 %collective-permute-start.1 = (bf16[1,256,1,128]{1,3,2,0:T(8,128)(2,1)S(1)}, bf16[1,256,1,128]{1,3,2,0:T(8,128)(2,1)S(1)}, u32[]{:S(2)}, u32[]{:S(2)}) collective-permute-start(bf16[1,256,1,128]{1,3,2,0:T(8,128)(2,1)S(1)} %copy.115), channel_id=1, source_target_pairs={{8,0},{16,8},{24,16},{32,24},{40,32},{48,40},{56,48},{64,56},{72,6... | collective-permute-start | bytes 196616 | tf_op jit(solution)/shard_map/ppermute | solution.py:11
  190.1 6.1 %collective-permute-start.2 = (bf16[2,256,1,128]{1,3,2,0:T(8,128)(2,1)S(1)}, bf16[2,256,1,128]{1,3,2,0:T(8,128)(2,1)S(1)}, u32[]{:S(2)}, u32[]{:S(2)}) collective-permute-start(bf16[2,256,1,128]{1,3,2,0:T(8,128)(2,1)S(1)} %pad_maximum_fusion.2), channel_id=1, source_target_pairs={{1,0},{2,1},{3,2},{4,3},{5,4},{6,5},{7,6},{9,8},{10,9},{11,10},{12... | collective-permute-start | bytes 393224 | tf_op jit(solution)/shard_map/ppermute | solution.py:11
Sparse Core Ops, SparseCore 0:
  19.0 50.8 all-gather.2
  169.5 135.3 all-gather.4
